TPU v7x, 256 devices: a whole 4x4x8 slice. The times are simulated.
256 devices in a mesh: prompt: 2 (over core), resp: 32 (over z_lo, y, x), head: 4 (over z_hi).
Axes of the slice: x: 4, y: 4, z: 8 (z_hi: 4, z_lo: 2; z = z_hi * 2 + z_lo), core: 2. Of those that a mesh axis runs over, the one named last changes fastest.
Arguments:
- prefix_hidden: bfloat16 [4096, 5120], P(('prompt', 'resp', 'head')), may hold values from -24 to 24
- w_key: bfloat16 [5120, 1024], P(None, 'head'), may hold values from -0.083496094 to 0.083496094
- w_value: bfloat16 [5120, 1024], P(None, 'head'), may hold values from -0.16699219 to 0.16699219
- queries: bfloat16 [128, 256, 5120], P(('prompt', 'resp'), None, 'head'), may hold values from -6 to 6
- resp_keys: bfloat16 [128, 256, 1024], P(('prompt', 'resp'), None, 'head'), may hold values from -6 to 6
- resp_values: bfloat16 [128, 256, 1024], P(('prompt', 'resp'), None, 'head'), may hold values from -15 to 15
- lengths: int32 [128], P(('prompt', 'resp')), may hold values from 1 to 256, as said below
- assign: int32 [128], P(('prompt', 'resp')), may hold values from 0 to 1, as said below
- grad_out: bfloat16 [128, 256, 5120], P(('prompt', 'resp'), None, 'head'), may hold values from -6 to 6
Outputs:
- attn_out: bfloat16 [128, 256, 5120], P(('prompt', 'resp'), None, 'head')
- grad_query: bfloat16 [128, 256, 5120], P(('prompt', 'resp'), None, 'head')
- grad_rkey: bfloat16 [128, 256, 1024], P(('prompt', 'resp'), None, 'head')
- grad_rvalue: bfloat16 [128, 256, 1024], P(('prompt', 'resp'), None, 'head')
- grad_wkey: float32 [5120, 1024], P(('prompt', 'resp'), 'head')
- grad_wvalue: float32 [5120, 1024], P(('prompt', 'resp'), 'head')
Inputs may be any that keep to these rules, and one draw needn't show every extreme that they name: Response r's live positions are 0 to lengths[r] - 1; some response has all 256. `assign`: in each block of 64 consecutive responses (one prompt group) every prompt number is named by exactly 32 responses.
All inputs are finite; a program needn't handle non-finite values.
Results may differ from a plain program's by a relative error of at most 0.033.
Values may be sent and summed in bfloat16 or wider, within the bound.
A program may use at most 128 MiB of HBM per device.

v0:
```python
import math

import jax
import jax.numpy as jnp
from jax import lax
from jax.sharding import PartitionSpec as P

QH = 40
KVH = 8
HD = 128
PLEN = 1024


NEG_FILL = -1e30


def head_pass(query_rows, grad_rows, key_rows, value_rows, visible, live_rows):
    scale_factor = 1.0 / math.sqrt(query_rows.shape[1])
    scores = (
        lax.dot_general(
            query_rows, key_rows, (((1,), (1,)), ((), ())), preferred_element_type=jnp.float32
        )
        * scale_factor
    )
    scores = jnp.where(visible, scores, NEG_FILL)
    row_top = jnp.max(scores, axis=1, keepdims=True)
    exponent = jnp.exp(scores - row_top)
    weights = exponent / jnp.sum(exponent, axis=1, keepdims=True)
    weights_low = weights.astype(jnp.bfloat16)
    output = jnp.dot(weights_low, value_rows, preferred_element_type=jnp.float32)
    attended = (output * live_rows).astype(jnp.bfloat16)
    grad_live = grad_rows * live_rows.astype(jnp.bfloat16)
    row_delta = jnp.sum(
        grad_live.astype(jnp.float32) * attended.astype(jnp.float32), axis=1, keepdims=True
    )
    grad_weights = lax.dot_general(
        grad_live, value_rows, (((1,), (1,)), ((), ())), preferred_element_type=jnp.float32
    )
    grad_scores = (weights * (grad_weights - row_delta) * scale_factor).astype(jnp.bfloat16)
    query_grad = jnp.dot(grad_scores, key_rows, preferred_element_type=jnp.float32).astype(
        jnp.bfloat16
    )
    key_grad = lax.dot_general(
        grad_scores, query_rows, (((0,), (0,)), ((), ())), preferred_element_type=jnp.float32
    )
    value_grad = lax.dot_general(
        weights_low, grad_live, (((0,), (0,)), ((), ())), preferred_element_type=jnp.float32
    )
    return (attended, query_grad, key_grad, value_grad)


def body(prefix_hidden, w_key, w_value, queries, resp_keys, resp_values, lengths, assign, grad_out):
    hidden_rows = lax.all_gather(prefix_hidden, "head", axis=0, tiled=True)
    projected = jnp.concatenate(
        [
            jnp.dot(hidden_rows, w_key, preferred_element_type=jnp.float32).astype(jnp.bfloat16),
            jnp.dot(hidden_rows, w_value, preferred_element_type=jnp.float32).astype(jnp.bfloat16),
        ],
        axis=1,
    )
    prefix_all = lax.all_gather(projected, "resp", axis=0, tiled=True)
    resp_count, resp_len, query_width = queries.shape
    kv_local = resp_keys.shape[2] // HD
    group_size = QH // KVH
    prompt_len = PLEN
    row_count = resp_len * group_size
    width_query = group_size * HD
    row_time = jnp.arange(row_count, dtype=jnp.int32) // group_size
    key_time = jnp.arange(resp_len, dtype=jnp.int32)

    def per_item(item_index):
        which_resp = item_index // kv_local
        which_head = item_index % kv_local
        length_now = lengths[which_resp]
        start_row = assign[which_resp] * prompt_len
        query_block = lax.dynamic_index_in_dim(queries, which_resp, 0, keepdims=False)
        grad_block = lax.dynamic_index_in_dim(grad_out, which_resp, 0, keepdims=False)
        key_block = lax.dynamic_index_in_dim(resp_keys, which_resp, 0, keepdims=False)
        value_block = lax.dynamic_index_in_dim(resp_values, which_resp, 0, keepdims=False)
        query_rows = lax.dynamic_slice_in_dim(
            query_block, which_head * width_query, width_query, 1
        ).reshape(row_count, HD)
        grad_rows = lax.dynamic_slice_in_dim(
            grad_block, which_head * width_query, width_query, 1
        ).reshape(row_count, HD)
        prefix_keys = lax.dynamic_slice(prefix_all, (start_row, which_head * HD), (prompt_len, HD))
        prefix_values = lax.dynamic_slice(
            prefix_all, (start_row, (kv_local + which_head) * HD), (prompt_len, HD)
        )
        key_rows = jnp.concatenate(
            [prefix_keys, lax.dynamic_slice_in_dim(key_block, which_head * HD, HD, 1)], axis=0
        )
        value_rows = jnp.concatenate(
            [prefix_values, lax.dynamic_slice_in_dim(value_block, which_head * HD, HD, 1)], axis=0
        )
        resp_ok = (key_time[None, :] <= row_time[:, None]) & (key_time[None, :] < length_now)
        visible = jnp.concatenate(
            [jnp.ones((row_count, prompt_len), dtype=jnp.bool_), resp_ok], axis=1
        )
        live_rows = (row_time < length_now).astype(jnp.float32)[:, None]
        return head_pass(query_rows, grad_rows, key_rows, value_rows, visible, live_rows)

    attended, query_grad, key_grad, value_grad = lax.map(
        per_item, jnp.arange(resp_count * kv_local, dtype=jnp.int32)
    )

    def to_layout(stacked):
        return (
            stacked.reshape(resp_count, kv_local, resp_len, -1)
            .transpose(0, 2, 1, 3)
            .reshape(resp_count, resp_len, -1)
        )

    attn_out = to_layout(attended)
    grad_query = to_layout(query_grad)
    grad_rkey = to_layout(key_grad[:, prompt_len:].astype(jnp.bfloat16))
    grad_rvalue = to_layout(value_grad[:, prompt_len:].astype(jnp.bfloat16))

    def prefix_layout(stacked):
        return (
            stacked.reshape(resp_count, kv_local, prompt_len, HD)
            .transpose(0, 2, 1, 3)
            .reshape(resp_count, prompt_len, kv_local * HD)
        )

    prefix_pieces = jnp.concatenate(
        [prefix_layout(key_grad[:, :prompt_len]), prefix_layout(value_grad[:, :prompt_len])], axis=2
    )
    partial_term = jnp.zeros((prefix_all.shape[0], prefix_pieces.shape[2]), jnp.float32)
    for resp_slot in range(resp_count):
        slot_start = assign[resp_slot] * prompt_len
        current = lax.dynamic_slice_in_dim(partial_term, slot_start, prompt_len, 0)
        partial_term = lax.dynamic_update_slice_in_dim(
            partial_term, current + prefix_pieces[resp_slot], slot_start, 0
        )
    owned_grads = lax.psum_scatter(
        partial_term.astype(jnp.bfloat16), "resp", scatter_dimension=0, tiled=True
    )
    weight_grads = lax.psum_scatter(
        lax.dot_general(
            hidden_rows, owned_grads, (((0,), (0,)), ((), ())), preferred_element_type=jnp.float32
        ),
        ("prompt", "resp"),
        scatter_dimension=0,
        tiled=True,
    )
    kv_width = kv_local * HD
    return (
        attn_out,
        grad_query,
        grad_rkey,
        grad_rvalue,
        weight_grads[:, :kv_width],
        weight_grads[:, kv_width:],
    )


def solution(mesh):
    return jax.shard_map(
        body,
        mesh=mesh,
        in_specs=(
            P(("prompt", "resp", "head"), None),
            P(None, "head"),
            P(None, "head"),
            P(("prompt", "resp"), None, "head"),
            P(("prompt", "resp"), None, "head"),
            P(("prompt", "resp"), None, "head"),
            P(("prompt", "resp")),
            P(("prompt", "resp")),
            P(("prompt", "resp"), None, "head"),
        ),
        out_specs=(
            P(("prompt", "resp"), None, "head"),
            P(("prompt", "resp"), None, "head"),
            P(("prompt", "resp"), None, "head"),
            P(("prompt", "resp"), None, "head"),
            P(("prompt", "resp"), "head"),
            P(("prompt", "resp"), "head"),
        ),
        check_vma=False,
    )
```

profile of v0, /device:TPU:160, one launch (start us, length us, event | category | flops | bytes accessed | tf_op | source)
XLA Modules:
  0.0 843.4 jit_solution(14977466364126825098)
XLA Ops:
  7.2 18.0 %all_gather.6 = bf16[64,5120]{1,0:T(8,128)(2,1)S(1)} all-gather(bf16[16,5120]{1,0:T(8,128)(2,1)} %param.11), channel_id=1, replica_groups=mesh['prompt'=2,'resp'=32,'head'=4] {'head'}, dimensions={0}, use_global_device_ids=true | all-gather | bytes 819200 | tf_op jit(solution)/shard_map/all_gather | solution.py:53
  29.0 154.3 %all-gather.2.cloned.1.call-done = bf16[2048,512]{1,0:T(8,128)(2,1)} async-done(((bf16[64,512]{1,0:T(8,128)(2,1)}), bf16[2048,512]{1,0:T(8,128)(2,1)}) %all-gather.2.cloned.1.call-update) | async-done | bytes 2097168 | tf_op jit(solution)/shard_map/all_gather | solution.py:61
  183.3 117.5 %while.21 = (s32[]{:T(128)}, bf16[4,1280,128]{2,1,0:T(8,128)(2,1)}, bf16[4,1280,128]{2,1,0:T(8,128)(2,1)}, f32[4,1280,128]{2,1,0:T(8,128)}, f32[4,1280,128]{2,1,...) while((s32[]{:T(128)}, bf16[4,1280,128]{2,1,0:T(8,128)(2,1)}, ...), condition=%wide.region_4.5_spmd.clone.clone, body=%wide.region_0.4_spmd.clone.clone.sunk | while | flops 2544455936 | bytes 64238080 | solution.py:103
  201.0 3.6 fusion.81
  208.2 2.7 fusion.82
  230.3 3.6 fusion.81
  237.5 2.7 fusion.82
  257.8 1.9 fusion.84
  259.7 3.6 fusion.81
  266.9 2.7 fusion.82
  289.0 3.6 fusion.81
  296.3 2.7 fusion.82
  300.8 3.1 slice.35
  303.9 1.9 copy.55
  305.8 3.1 slice.34
  308.9 2.9 copy.54
  314.5 2.7 copy.60
  317.3 165.9 %reduce-scatter.7.cloned.1.call-done = bf16[64,512]{1,0:T(8,128)(2,1)} async-done(((bf16[2048,512]{1,0:T(8,128)(2,1)}), bf16[64,512]{1,0:T(8,128)(2,1)}) %reduce-scatter.7.cloned.1.call-update) | async-done | bytes 65552
  483.2 6.2 convolution_bitcast_fusion.2
  489.5 11.4 %copy.62 = f32[5120,512]{1,0:T(8,128)} copy(f32[5120,512]{0,1:T(8,128)} %convolution_bitcast_fusion.2) | data formatting | bytes 20971520
  508.5 3.6 reshape.104
  512.2 3.7 copy.71
  515.9 4.2 reshape.105
  520.2 315.1 %reduce-scatter.9.cloned.1.call-done = f32[80,512]{1,0:T(8,128)} async-done(((f32[5120,512]{1,0:T(8,128)}), f32[80,512]{1,0:T(8,128)}) %reduce-scatter.9.cloned.1.call-update) | async-done | bytes 163856
  (194 shorter events, 91.0 us)
Async XLA Ops:
  7.2 18.1 %copy-start = (bf16[5120,256]{1,0:T(8,128)(2,1)S(1)}, bf16[5120,256]{1,0:T(8,128)(2,1)}, u32[]{:S(2)}) copy-start(bf16[5120,256]{1,0:T(8,128)(2,1)} %param.13) | copy-start | bytes 7864324
  7.2 176.1 %all-gather.2.cloned.1.call-start = ((), (), s32[]{:S(2)}) async-start(), calls=%async_computation.2 | async-start | bytes 2162688 | tf_op jit(solution)/shard_map/all_gather | solution.py:61
  7.2 18.6 %copy-start.10 = (bf16[5120,256]{1,0:T(8,128)(2,1)S(1)}, bf16[5120,256]{1,0:T(8,128)(2,1)}, u32[]{:S(2)}) copy-start(bf16[5120,256]{1,0:T(8,128)(2,1)} %param.12) | copy-start | bytes 7864324
  25.2 158.1 %copy-start.16 = (s32[2]{0:T(128)S(1)}, s32[2]{0:T(128)}, u32[]{:S(2)}) copy-start(s32[2]{0:T(128)} %param.17) | copy-start | bytes 28
  27.0 456.2 %reduce-scatter.7.cloned.1.call-start = ((), (), s32[]{:S(2)}) async-start(), calls=%async_computation.3 | async-start | bytes 2162688
  190.8 4.7 copy-start.11
  190.8 6.8 copy-start.12
  192.2 5.5 copy-start.8
  194.2 4.9 copy-start.4
  220.1 4.7 copy-start.11
  220.1 6.8 copy-start.12
  221.5 5.4 copy-start.8
  223.5 4.9 copy-start.4
  249.5 4.7 copy-start.11
  249.5 6.8 copy-start.12
  250.9 5.5 copy-start.8
  252.9 4.9 copy-start.4
  278.9 4.7 copy-start.11
  278.9 6.8 copy-start.12
  280.3 5.4 copy-start.8
  282.2 4.9 copy-start.4
  314.5 168.7 %copy-start.7 = (bf16[64,5120]{1,0:T(8,128)(2,1)S(1)}, bf16[64,5120]{1,0:T(8,128)(2,1)}, u32[]{:S(2)}) copy-start(bf16[64,5120]{1,0:T(8,128)(2,1)} %copy-done.6) | copy-start | bytes 1966084
  317.2 518.0 %reduce-scatter.9.cloned.1.call-start = ((), (), s32[]{:S(2)}) async-start(), calls=%async_computation.4 | async-start | bytes 10649600
  508.5 328.3 %copy-start.1 = (bf16[5120,256]{1,0:T(8,128)(2,1)S(1)}, bf16[5120,256]{1,0:T(8,128)(2,1)}, u32[]{:S(2)}) copy-start(bf16[5120,256]{1,0:T(8,128)(2,1)} %param.13) | copy-start | bytes 7864324
  (20 other events, 37.1 us)
Sparse Core Ops, SparseCore 0:
  27.1 156.1 all-gather.1
  317.4 165.8 reduce-scatter.6
  501.0 334.2 reduce-scatter.8
where the time goes:
time: 845 us; the launch traced here: 843 us
  waiting for transfers between devices  635 us (75%)
  local copies, waits for them, and re-layouts  87.1 us (10%)
  matrix products  57.3 us (7%)
  blocking collectives  18 us (2%)
  other arithmetic  16.4 us (2%)
  between operations  15.3 us (2%)
  loops' own time  13.8 us (2%)
    unnamed x5, waiting for transfers between devices  481 us
    all_gather x1, waiting for transfers between devices, body(): prefix_all = lax.all_gather(projected, 'resp', axis=0, tiled=True)  154 us
    all_gather x1, blocking collectives, body(): hidden_rows = lax.all_gather(prefix_hidden, 'head', axis=0, tiled=True)  18 us
  transfers between devices with their start and end apart: 3, of which 3 were waited for; matrix products, arithmetic and copies ran while one was open for 2% of the time, Pallas kernels for 0%

commit v1 on v0

v1 whole, which is shorter than its diff:
```python
import math

import jax
import jax.numpy as jnp
from jax import lax
from jax.experimental import pallas as pl
from jax.experimental.pallas import tpu as pltpu
from jax.sharding import PartitionSpec as P

HD = 128
PLEN = 1024
RLEN = 256
GRP = 5
NX = NY = 4
NZ = 2
NEG_FILL = -1e30
SCALE = 1.0 / math.sqrt(HD)
SCALE_LOG2E = SCALE * math.log2(math.e)
NT = (((1,), (1,)), ((), ()))
TN = (((0,), (0,)), ((), ()))
MESH = pl.DeviceIdType.MESH
F32 = jnp.float32
B16 = jnp.bfloat16
VMEM_LIMIT = 56 * 2**20


PLANE = ((0, 1), (0, 3), (1, 0), (1, 1), (1, 3), (0, 2), (1, 2))
RING = (1, 3, 2)
BLOCKS = 4


class Place:
    def __init__(self):
        self.p = lax.axis_index("prompt")
        self.r = lax.axis_index("resp")
        self.h = lax.axis_index("head")
        self.z = self.r // (NY * NX)
        self.y = lax.rem(self.r // NX, NY)
        self.x = lax.rem(self.r, NX)
        self.zs = [self.z, 1 - self.z]
        self.ys = [lax.rem(self.y + s, NY) for s in range(NY)]
        self.xs = [lax.rem(self.x + s, NX) for s in range(NX)]
        self.core = (1 - self.p, self.r, self.h)
        self.head = [(self.p, self.r, lax.rem(self.h + s, 4)) for s in range(4)]
        steps = [(0, s, 0) for s in range(NY)] + [(0, 0, s) for s in range(1, NX)]
        steps += [(1, s, 0) for s in range(NY)] + [(1, 0, s) for s in range(1, NX)]
        steps += [(0, s, t) for s in range(1, NY) for t in range(1, NX)]
        self.to = {
            (dz, dy, dx): (self.p, (self.zs[dz] * NY + self.ys[dy]) * NX + self.xs[dx], self.h)
            for dz, dy, dx in steps
        }

    def peers(self):
        return [self.core, self.head[1], self.head[3]] + [t for s, t in self.to.items() if s != (0, 0, 0)]


class Links:
    def __init__(self, send_sem, recv_sem):
        self.send_sem, self.recv_sem = send_sem, recv_sem
        self.count = 0

    def copy(self, number, src, dst, target):
        return pltpu.make_async_remote_copy(
            src_ref=src, dst_ref=dst, send_sem=self.send_sem.at[number],
            recv_sem=self.recv_sem.at[number], device_id=target, device_id_type=MESH,
        )

    def send(self, src, dst, target):
        number = self.count
        self.count += 1
        self.copy(number, src, dst, target).start()
        return number

    def landed(self, number, region, target):
        self.copy(number, region, region, target).wait()


def greet(peers):
    barrier = pltpu.get_barrier_semaphore()
    for peer in peers:
        pl.semaphore_signal(barrier, inc=1, device_id=peer, device_id_type=MESH)
    pl.semaphore_wait(barrier, len(peers))


def step_of(axis, dz, s):
    return (dz, s, 0) if axis == "y" else (dz, 0, s)


def along(place, axis, s):
    return (place.ys if axis == "y" else place.xs)[s]


def gather_rows(links, place, kview, vview):
    every = slice(None)
    sent = []
    for dz, s in PLANE:
        for axis, view in (("y", kview), ("x", vview)):
            own = view(place.z, place.y, place.x)
            sent.append((links.send(own, own, place.to[step_of(axis, dz, s)]), dz, s, axis, view))
    yield
    for number, dz, s, axis, view in sent:
        z, k = place.zs[dz], along(place, axis, (4 - s) % 4)
        region = view(z, k, place.x) if axis == "y" else view(z, place.y, k)
        links.landed(number, region, place.to[step_of(axis, dz, (4 - s) % 4)])
    sent = []
    for s in RING:
        for axis, view in (("x", kview), ("y", vview)):
            own = view(every, every, place.x) if axis == "x" else view(every, place.y, every)
            sent.append((links.send(own, own, place.to[step_of(axis, 0, s)]), s, axis, view))
    yield
    for number, s, axis, view in sent:
        k = along(place, axis, 4 - s)
        region = view(every, every, k) if axis == "x" else view(every, k, every)
        links.landed(number, region, place.to[step_of(axis, 0, 4 - s)])


def reduce_rows(links, place, kterm, vterm, buf1, buf2, mid, put):
    every = slice(None)
    sent = []
    for s in RING:
        for which, axis, term in ((0, "x", kterm), (1, "y", vterm)):
            k = along(place, axis, s)
            src = term(every, every, k) if axis == "x" else term(every, k, every)
            sent.append((links.send(src, buf1.at[which, s - 1], place.to[step_of(axis, 0, s)]), which, s, axis))
    yield
    for number, which, s, axis in sent:
        links.landed(number, buf1.at[which, s - 1], place.to[step_of(axis, 0, 4 - s)])
    for which, own in ((0, kterm(every, every, place.x)), (1, vterm(every, place.y, every))):
        total = own[...].astype(F32)
        for s in range(3):
            total = total + buf1[which, s].astype(F32)
        mid[which] = total.astype(B16)
    sent = []
    for i, (dz, s) in enumerate(PLANE):
        for which, axis in ((0, "y"), (1, "x")):
            src = mid.at[which, place.zs[dz], along(place, axis, s)]
            sent.append((links.send(src, buf2.at[which, i], place.to[step_of(axis, dz, s)]), which, i, axis, dz, s))
    yield
    for number, which, i, axis, dz, s in sent:
        links.landed(number, buf2.at[which, i], place.to[step_of(axis, dz, (4 - s) % 4)])
    for which, k in ((0, place.y), (1, place.x)):
        total = mid[which, place.z, k].astype(F32)
        for i in range(len(PLANE)):
            total = total + buf2[which, i].astype(F32)
        put(which, total.astype(B16))


def swap_columns(links, place, hall, mine, turned, cols):
    half = hall.shape[1] // 2
    width = half // NZ
    partner = place.to[(1, 0, 0)]
    sent = []
    for p in range(2):
        theirs = pl.ds(pl.multiple_of(p * half + place.zs[1] * width, width), width)
        sent.append((links.send(hall.at[:, theirs], mine.at[p, place.z], partner), p))
        ours = pl.ds(pl.multiple_of(p * half + place.z * width, width), width)
        mine[p, place.z] = hall[:, ours]
    yield
    for number, p in sent:
        links.landed(number, mine.at[p, place.zs[1]], partner)
    for p in range(2):
        block = mine[p].reshape(mine.shape[1] * mine.shape[2], width)
        turned[p] = block.T.reshape(turned.shape[1:])
    sent = []
    for dy in range(NY):
        for dx in range(NX):
            if dy or dx:
                number = links.send(
                    turned.at[:, place.ys[dy], place.xs[dx]], cols.at[place.y, place.x], place.to[(0, dy, dx)]
                )
                sent.append((number, dy, dx))
    for p in range(2):
        cols[place.y, place.x, p] = turned[p, place.y, place.x]
    yield
    for number, dy, dx in sent:
        dy, dx = (4 - dy) % 4, (4 - dx) % 4
        links.landed(number, cols.at[place.ys[dy], place.xs[dx]], place.to[(0, dy, dx)])


def layer_kernel(lengths, assign, hid, wk_hbm, wv_hbm, q_hbm, do_hbm, rk_hbm, rv_hbm,
                 o_hbm, dq_hbm, drk_hbm, drv_hbm, wk_out, wv_out,
                 hall, wk, wv, kbuf, vbuf, mine, turned, cols, lhs,
                 qb, gb, kall, vall, ob, dqb, drk, drv, dsb, erb, acck, accv, gk, gv,
                 buf1, buf2, mid, gsum, theirs, landing,
                 w_sem, in_sem, out_sem, send_sem, recv_sem):
    place = Place()
    links = Links(send_sem, recv_sem)
    wide = GRP * HD

    def part(ref, b, width):
        return ref.at[b % 2, :, pl.ds((b // 2) * width, width)]

    w_loads = [pltpu.make_async_copy(s, d, w_sem.at[i]) for i, (s, d) in enumerate(((wk_hbm, wk), (wv_hbm, wv)))]
    loads = []
    for b in range(BLOCKS):
        pairs = ((part(q_hbm, b, wide), qb.at[b]), (part(do_hbm, b, wide), gb.at[b]),
                 (part(rk_hbm, b, HD), kall.at[b, pl.ds(PLEN, RLEN)]), (part(rv_hbm, b, HD), vall.at[b, pl.ds(PLEN, RLEN)]))
        loads += [pltpu.make_async_copy(s, d, in_sem.at[4 * b + i]) for i, (s, d) in enumerate(pairs)]
    for load in w_loads + loads:
        load.start()
    greet(place.peers())

    to_left, to_right = place.head[3], place.head[1]
    half = hid.shape[1] // 2
    lo, hi = pl.ds(0, half), pl.ds(half, half)
    low, high, far = (pl.ds(s, 16) for s in (16, 32, 48))
    a = links.send(hid.at[:, lo], hall.at[low, lo], to_right)
    b = links.send(hid.at[:, hi], hall.at[high, hi], to_left)
    c = links.send(hid.at[:, hi], hall.at[low, hi], to_right)
    d = links.send(hid.at[:, lo], hall.at[high, lo], to_left)
    hall[0:16] = hid[...]
    for load in w_loads:
        load.wait()

    def project(start, size):
        rows = hall[start:start + size]
        for w, out in ((wk, kbuf), (wv, vbuf)):
            block = jnp.dot(rows, w[...], preferred_element_type=F32).astype(B16)
            for g in range(2):
                out[g, place.z, place.y, place.x, start:start + size] = block[:, g * HD:(g + 1) * HD]

    def gather(start, size, g):
        rows = pl.ds(start, size)
        return gather_rows(
            links, place,
            lambda z, y, x: kbuf.at[g, z, y, x, rows],
            lambda z, y, x: vbuf.at[g, z, y, x, rows],
        )

    every = slice(None)
    project(0, 16)
    first = gather(0, 16, every)
    next(first)
    links.landed(a, hall.at[low, lo], to_left)
    e = links.send(hall.at[low, lo], hall.at[far, lo], to_right)
    links.landed(b, hall.at[high, hi], to_right)
    f = links.send(hall.at[high, hi], hall.at[far, hi], to_left)
    next(first)
    links.landed(c, hall.at[low, hi], to_left)
    links.landed(d, hall.at[high, lo], to_right)
    project(16, 32)
    second = gather(16, 32, every)
    next(second)
    links.landed(e, hall.at[far, lo], to_left)
    links.landed(f, hall.at[far, hi], to_right)
    project(48, 16)
    third, fourth = gather(48, 16, 0), gather(48, 16, 1)
    next(third)
    next(second)
    next(fourth)
    swap = swap_columns(links, place, hall, mine, turned, cols)
    next(swap)
    for load in loads:
        load.wait()
    next(first, None)
    next(third)
    next(second, None)
    next(third, None)

    def terms(ref, g):
        return lambda z, y, x: ref.at[g, z, y, x]

    def put(g):
        def store(which, total):
            gsum[g, place.y, place.x, place.z, :, which * HD:(which + 1) * HD] = total
        return store

    def reduce(g):
        return reduce_rows(links, place, terms(gk, g), terms(gv, g), buf1.at[g], buf2.at[g], mid.at[g], put(g))

    def regather(g):
        return gather_rows(
            links, place,
            lambda z, y, x: gsum.at[g, y, x, z, :, pl.ds(0, HD)],
            lambda z, y, x: gsum.at[g, y, x, z, :, pl.ds(HD, HD)],
        )

    reduces = [reduce(0), reduce(1)]
    causal = lax.broadcasted_iota(jnp.int32, (RLEN, RLEN), 1) <= lax.broadcasted_iota(jnp.int32, (RLEN, RLEN), 0)

    def block(b, _):
        g, r = b // 2, lax.rem(b, 2)

        @pl.when(b == 1)
        def _():
            next(fourth)
            next(swap)

        @pl.when(b == 2)
        def _():
            next(reduces[0])
            next(fourth, None)

        is_first = assign[r] == 0
        live = lax.broadcasted_iota(jnp.int32, (RLEN, 1), 0) < lengths[r]
        for src, dst in ((kbuf, kall), (vbuf, vall)):
            dst[b, :PLEN] = jnp.where(is_first, src[g, 0].reshape(PLEN, HD), src[g, 1].reshape(PLEN, HD))
        dkt = dvt = None
        for j in range(GRP):
            lanes = slice(j * HD, (j + 1) * HD)
            q = qb[b, :, lanes]
            k = kall[b]
            v = vall[b]
            s = lax.dot_general(q, k, NT, preferred_element_type=F32)
            s = jnp.concatenate([s[:, :PLEN], jnp.where(causal, s[:, PLEN:], NEG_FILL)], axis=1)
            top = jnp.max(s, axis=1, keepdims=True)
            e = jnp.exp2((s - top) * SCALE_LOG2E)
            inv = 1.0 / jnp.sum(e, axis=1, keepdims=True)
            inv = jnp.where(live, inv, 0.0)
            e_low = e.astype(B16)
            out = (jnp.dot(e_low, v, preferred_element_type=F32) * inv).astype(B16)
            ob[b, :, lanes] = out
            grad = (gb[b, :, lanes].astype(F32) * inv).astype(B16)
            gb[b, :, lanes] = grad
            delta = jnp.sum(grad.astype(F32) * out.astype(F32), axis=1, keepdims=True)
            dp = lax.dot_general(grad, v, NT, preferred_element_type=F32)
            ds = (e * (dp - delta)).astype(B16)
            dsb[b, j] = ds
            erb[b, j] = e_low[:, PLEN:]
            kt = lax.dot_general(q, ds[:, :PLEN], TN, preferred_element_type=F32)
            vt = lax.dot_general(grad, e_low[:, :PLEN], TN, preferred_element_type=F32)
            dkt = kt if j == 0 else dkt + kt
            dvt = vt if j == 0 else dvt + vt
            if j == 2:
                @pl.when(b == 3)
                def _():
                    next(reduces[0])
        dk = (dkt * SCALE).T
        dv = dvt.T

        @pl.when(r == 0)
        def _():
            for i in range(2):
                mine_too = is_first if i == 0 else jnp.logical_not(is_first)
                acck[i] = jnp.where(mine_too, dk, 0.0)
                accv[i] = jnp.where(mine_too, dv, 0.0)

        @pl.when(r == 1)
        def _():
            for i in range(2):
                mine_too = is_first if i == 0 else jnp.logical_not(is_first)
                shape = gk.shape[2:]
                gk[g, i] = (acck[i] + jnp.where(mine_too, dk, 0.0)).astype(B16).reshape(shape)
                gv[g, i] = (accv[i] + jnp.where(mine_too, dv, 0.0)).astype(B16).reshape(shape)

        return 0

    lax.fori_loop(0, BLOCKS, block, 0)

    stores = []

    def store(number, src, dst):
        copy = pltpu.make_async_copy(src, dst, out_sem.at[number])
        copy.start()
        stores.append(copy)

    def late(b):
        dkt = dvt = None
        for j in range(GRP):
            lanes = slice(j * HD, (j + 1) * HD)
            dqb[b, :, lanes] = (jnp.dot(dsb[b, j], kall[b], preferred_element_type=F32) * SCALE).astype(B16)
            kt = lax.dot_general(qb[b, :, lanes], dsb[b, j, :, PLEN:], TN, preferred_element_type=F32)
            vt = lax.dot_general(gb[b, :, lanes], erb[b, j], TN, preferred_element_type=F32)
            dkt = kt if j == 0 else dkt + kt
            dvt = vt if j == 0 else dvt + vt
        drk[b] = (dkt * SCALE).T.astype(B16)
        drv[b] = dvt.T.astype(B16)
        store(4 * b, ob.at[b], part(o_hbm, b, wide))
        store(4 * b + 1, dqb.at[b], part(dq_hbm, b, wide))
        store(4 * b + 2, drk.at[b], part(drk_hbm, b, HD))
        store(4 * b + 3, drv.at[b], part(drv_hbm, b, HD))

    count = cols.shape[3]

    def product(g):
        rhs = gsum[g].reshape(NY * NX * NZ * gsum.shape[4], 2 * HD)
        theirs[g] = jnp.dot(lhs[...], rhs, preferred_element_type=F32).reshape(2, count, 2 * HD)
        return links.send(theirs.at[g, 1 - place.p], landing.at[g], place.core)

    def finish(g, number):
        links.landed(number, landing.at[g], place.core)
        total = theirs[g, place.p] + landing[g]
        wk_out[:, g * HD:(g + 1) * HD] = total[:, :HD]
        wv_out[:, g * HD:(g + 1) * HD] = total[:, HD:]

    next(reduces[1])
    late(0)
    next(reduces[0], None)
    regathers = [regather(0), regather(1)]
    next(regathers[0])
    late(1)
    next(swap, None)
    for y in range(NY):
        for x in range(NX):
            at = (y * NX + x) * HD
            lhs[:, at:at + HD] = cols[y, x].reshape(2 * count, HD)
    next(reduces[1])
    next(regathers[0])
    late(2)
    next(reduces[1], None)
    next(regathers[1])
    late(3)
    next(regathers[1])
    next(regathers[0], None)
    first_product = product(0)
    next(regathers[1], None)
    second_product = product(1)
    finish(0, first_product)
    finish(1, second_product)
    for copy in stores:
        copy.wait()


def layer(prefix_hidden, w_key, w_value, queries, resp_keys, resp_values, lengths, assign, grad_out):
    rows, depth = prefix_hidden.shape
    width = w_key.shape[1]
    count = depth // (2 * NZ * NY * NX)
    tall = 4 * rows
    S = jax.ShapeDtypeStruct
    vm = pl.BlockSpec(memory_space=pltpu.VMEM)
    sm = pl.BlockSpec(memory_space=pltpu.SMEM)
    hbm = pl.BlockSpec(memory_space=pl.ANY)
    V = pltpu.VMEM
    keys = PLEN + RLEN
    wide = GRP * HD
    copies = 192
    grads = S((count, width), F32)
    return pl.pallas_call(
        layer_kernel,
        in_specs=[sm, sm, vm] + [hbm] * 6,
        out_specs=[hbm] * 4 + [vm] * 2,
        out_shape=[S(queries.shape, B16), S(queries.shape, B16), S(resp_keys.shape, B16), S(resp_keys.shape, B16), grads, grads],
        scratch_shapes=[
            V((tall, depth), B16), V((depth, width), B16), V((depth, width), B16),
            V((2, NZ, NY, NX, tall, HD), B16), V((2, NZ, NY, NX, tall, HD), B16),
            V((2, NZ, tall, depth // 4), B16), V((2, NY, NX, count, HD), B16),
            V((NY, NX, 2, count, HD), B16), V((2 * count, NY * NX * HD), B16),
            V((BLOCKS, RLEN, wide), B16), V((BLOCKS, RLEN, wide), B16),
            V((BLOCKS, keys, HD), B16), V((BLOCKS, keys, HD), B16),
            V((BLOCKS, RLEN, wide), B16), V((BLOCKS, RLEN, wide), B16),
            V((BLOCKS, RLEN, HD), B16), V((BLOCKS, RLEN, HD), B16),
            V((BLOCKS, GRP, RLEN, keys), B16), V((BLOCKS, GRP, RLEN, RLEN), B16),
            V((2, PLEN, HD), F32), V((2, PLEN, HD), F32),
            V((2, NZ, NY, NX, tall, HD), B16), V((2, NZ, NY, NX, tall, HD), B16),
            V((2, 2, 3, NZ, 4, tall, HD), B16), V((2, 2, 7, tall, HD), B16), V((2, 2, NZ, 4, tall, HD), B16),
            V((2, NY, NX, NZ, tall, 2 * HD), B16),
            V((2, 2, count, 2 * HD), F32), V((2, count, 2 * HD), F32),
            pltpu.SemaphoreType.DMA((2,)), pltpu.SemaphoreType.DMA((4 * BLOCKS,)), pltpu.SemaphoreType.DMA((4 * BLOCKS,)),
            pltpu.SemaphoreType.DMA((copies,)), pltpu.SemaphoreType.DMA((copies,)),
        ],
        compiler_params=pltpu.CompilerParams(collective_id=0, has_side_effects=True, vmem_limit_bytes=VMEM_LIMIT),
        name="layer",
    )(lengths, assign, prefix_hidden, w_key, w_value, queries, grad_out, resp_keys, resp_values)


def hand_over_kernel(*refs):
    count = (len(refs) - 2) // 3
    sources, targets, held = refs[:count], refs[count:2 * count], refs[2 * count:3 * count]
    in_sem, out_sem = refs[3 * count:]
    reads, writes = [], []
    for i in range(count):
        for part in range(2):
            rows = pl.ds(part * (sources[i].shape[0] // 2), sources[i].shape[0] // 2)
            number = 2 * i + part
            reads.append(pltpu.make_async_copy(sources[i].at[rows], held[i].at[rows], in_sem.at[number]))
            writes.append(pltpu.make_async_copy(held[i].at[rows], targets[i].at[rows], out_sem.at[number]))
    for copy in reads:
        copy.start()
    for read, write in zip(reads, writes):
        read.wait()
        write.start()
    for copy in writes:
        copy.wait()


def hand_over(*arrays):
    hbm = pl.BlockSpec(memory_space=pl.ANY)
    return pl.pallas_call(
        hand_over_kernel,
        in_specs=[hbm] * len(arrays),
        out_specs=[hbm] * len(arrays),
        out_shape=[jax.ShapeDtypeStruct(a.shape, a.dtype) for a in arrays],
        scratch_shapes=[pltpu.VMEM(a.shape, a.dtype) for a in arrays]
        + [pltpu.SemaphoreType.DMA((2 * len(arrays),)), pltpu.SemaphoreType.DMA((2 * len(arrays),))],
        name="hand_over",
    )(*arrays)


def body(*arrays):
    return tuple(hand_over(*layer(*arrays)))


def solution(mesh):
    return jax.shard_map(
        body,
        mesh=mesh,
        in_specs=(
            P(("prompt", "resp", "head"), None),
            P(None, "head"),
            P(None, "head"),
            P(("prompt", "resp"), None, "head"),
            P(("prompt", "resp"), None, "head"),
            P(("prompt", "resp"), None, "head"),
            P(("prompt", "resp")),
            P(("prompt", "resp")),
            P(("prompt", "resp"), None, "head"),
        ),
        out_specs=(
            P(("prompt", "resp"), None, "head"),
            P(("prompt", "resp"), None, "head"),
            P(("prompt", "resp"), None, "head"),
            P(("prompt", "resp"), None, "head"),
            P(("prompt", "resp"), "head"),
            P(("prompt", "resp"), "head"),
        ),
        check_vma=False,
    )
```

time: 845 us -> 98.4 us (0.12)
  the two profiles are of different devices: /device:TPU:160 before, /device:TPU:1 now
where the time goes in v1:
time: 98.4 us; the launch traced here: 98.2 us
  Pallas kernels  97.4 us (99%)
    pallas_call x1, Pallas kernels, layer(): pl.pallas_call(layer_kernel, in_specs=[sm, sm, vm] + [hbm] * 6, out_specs...  94.5 us
    pallas_call x1, Pallas kernels, hand_over(): pl.pallas_call(hand_over_kernel, in_specs=[hbm] * len(arrays), out_specs=...  2.99 us

profile of v1, /device:TPU:1, one launch (start us, length us, event | category | flops | bytes accessed | tf_op | source)
XLA Modules:
  0.0 98.2 jit_solution(6648370426686141125)
XLA Ops:
  0.6 94.5 %layer.1 = (bf16[2,256,1280]{2,1,0:T(8,128)(2,1)}, bf16[2,256,1280]{2,1,0:T(8,128)(2,1)}, bf16[2,256,256]{2,1,0:T(8,128)(2,1)}, bf16[2,256,256]{2,1,0:T(8,128)(2...) custom-call(s32[2]{0:T(128)} %lengths.1, s32[2]{0:T(128)} %assign.1, bf16[16,5120]{1,0:T(8,128)(2,1)} %hid.1, ...), custom_call_target="tpu_custom_call" | custom-call | tf_op jit(solution)/shard_map/layer/pallas_call | solution.py:428
  95.1 3.0 %hand_over.1 = (bf16[2,256,1280]{2,1,0:T(8,128)(2,1)}, bf16[2,256,1280]{2,1,0:T(8,128)(2,1)}, bf16[2,256,256]{2,1,0:T(8,128)(2,1)}, bf16[2,256,256]{2,1,0:T(8,12...) custom-call(bf16[2,256,1280]{2,1,0:T(8,128)(2,1)} %get-tuple-element.12.refs_0_, ...), custom_call_target="tpu_custom_call" | custom-call | tf_op jit(solution)/shard_map/hand_over/pallas_call | solution.py:478

commit v2 on v1

--- a/solution.py
+++ b/solution.py
@@ -40,18 +40,20 @@
         self.zs = [self.z, 1 - self.z]
         self.ys = [lax.rem(self.y + s, NY) for s in range(NY)]
         self.xs = [lax.rem(self.x + s, NX) for s in range(NX)]
+        self.cores = [self.p, 1 - self.p]
         self.core = (1 - self.p, self.r, self.h)
         self.head = [(self.p, self.r, lax.rem(self.h + s, 4)) for s in range(4)]
         steps = [(0, s, 0) for s in range(NY)] + [(0, 0, s) for s in range(1, NX)]
         steps += [(1, s, 0) for s in range(NY)] + [(1, 0, s) for s in range(1, NX)]
-        steps += [(0, s, t) for s in range(1, NY) for t in range(1, NX)]
         self.to = {
             (dz, dy, dx): (self.p, (self.zs[dz] * NY + self.ys[dy]) * NX + self.xs[dx], self.h)
             for dz, dy, dx in steps
         }
 
     def peers(self):
-        return [self.core, self.head[1], self.head[3]] + [t for s, t in self.to.items() if s != (0, 0, 0)]
+        near = [t for s, t in self.to.items() if s != (0, 0, 0)]
+        across = [(self.cores[1], *self.to[step_of(axis, 0, s)][1:]) for axis in "xy" for s in RING]
+        return [self.core, self.head[1], self.head[3]] + near + across
 
 
 class Links:
@@ -112,6 +114,65 @@
         k = along(place, axis, 4 - s)
         region = view(every, every, k) if axis == "x" else view(every, k, every)
         links.landed(number, region, place.to[step_of(axis, 0, 4 - s)])
+
+
+def gather_rows_late(links, place, kview, vview):
+    every = slice(None)
+    partner = place.to[(1, 0, 0)]
+    sent = []
+    for view in (kview, vview):
+        own = view(place.z, place.y, place.x)
+        sent.append((links.send(own, own, partner), view))
+    yield
+    for number, view in sent:
+        links.landed(number, view(place.zs[1], place.y, place.x), partner)
+    for stage in range(2):
+        sent = []
+        for s in RING:
+            for axis, view in (("yx"[stage], kview), ("xy"[stage], vview)):
+                def region(k, axis=axis, view=view):
+                    if stage == 0:
+                        return view(every, k, place.x) if axis == "y" else view(every, place.y, k)
+                    return view(every, k, every) if axis == "y" else view(every, every, k)
+                own = region(along(place, axis, 0))
+                sent.append((links.send(own, own, place.to[step_of(axis, 0, s)]), s, axis, region))
+        yield
+        for number, s, axis, region in sent:
+            links.landed(number, region(along(place, axis, 4 - s)), place.to[step_of(axis, 0, 4 - s)])
+
+
+def gather_plane(links, place, kview, vview):
+    sent = []
+    for dz, s in PLANE:
+        for axis, view in (("y", kview), ("x", vview)):
+            own = view(place.z, along(place, axis, 0))
+            sent.append((links.send(own, own, place.to[step_of(axis, dz, s)]), dz, s, axis, view))
+    yield
+    for number, dz, s, axis, view in sent:
+        back = (4 - s) % 4
+        links.landed(number, view(place.zs[dz], along(place, axis, back)), place.to[step_of(axis, dz, back)])
+
+
+def reduce_products(links, place, theirs, landing, done):
+    sent = []
+    for s in (2, 1, 3, 0):
+        for core in (1, 0):
+            if core or s:
+                for which, axis in ((0, "x"), (1, "y")):
+                    slot = 4 * core + s - 1
+                    target = place.to[step_of(axis, 0, s)]
+                    target = (place.cores[core], *target[1:])
+                    number = links.send(theirs.at[which, core, s], landing.at[which, slot], target)
+                    sent.append((number, which, axis, s, core, slot))
+    yield
+    for number, which, axis, s, core, slot in sent:
+        target = place.to[step_of(axis, 0, (4 - s) % 4)]
+        links.landed(number, landing.at[which, slot], (place.cores[core], *target[1:]))
+    for which in range(2):
+        total = theirs[which, 0, 0].astype(F32)
+        for slot in range(7):
+            total = total + landing[which, slot].astype(F32)
+        done(which, total)
 
 
 def reduce_rows(links, place, kterm, vterm, buf1, buf2, mid, put):
@@ -162,26 +223,25 @@
         block = mine[p].reshape(mine.shape[1] * mine.shape[2], width)
         turned[p] = block.T.reshape(turned.shape[1:])
     sent = []
-    for dy in range(NY):
-        for dx in range(NX):
-            if dy or dx:
-                number = links.send(
-                    turned.at[:, place.ys[dy], place.xs[dx]], cols.at[place.y, place.x], place.to[(0, dy, dx)]
-                )
-                sent.append((number, dy, dx))
+    for s in RING:
+        for which, axis in ((0, "y"), (1, "x")):
+            src = turned.at[:, place.ys[s]] if axis == "y" else turned.at[:, :, place.xs[s]]
+            number = links.send(src, cols.at[which, along(place, axis, 0)], place.to[step_of(axis, 0, s)])
+            sent.append((number, which, axis, s))
     for p in range(2):
-        cols[place.y, place.x, p] = turned[p, place.y, place.x]
-    yield
-    for number, dy, dx in sent:
-        dy, dx = (4 - dy) % 4, (4 - dx) % 4
-        links.landed(number, cols.at[place.ys[dy], place.xs[dx]], place.to[(0, dy, dx)])
+        cols[0, place.y, p] = turned[p, place.y]
+        for k in range(4):
+            cols[1, place.x, p, k] = turned[p, k, place.x]
+    yield
+    for number, which, axis, s in sent:
+        links.landed(number, cols.at[which, along(place, axis, 4 - s)], place.to[step_of(axis, 0, 4 - s)])
 
 
 def layer_kernel(lengths, assign, hid, wk_hbm, wv_hbm, q_hbm, do_hbm, rk_hbm, rv_hbm,
                  o_hbm, dq_hbm, drk_hbm, drv_hbm, wk_out, wv_out,
                  hall, wk, wv, kbuf, vbuf, mine, turned, cols, lhs,
                  qb, gb, kall, vall, ob, dqb, drk, drv, dsb, erb, acck, accv, gk, gv,
-                 buf1, buf2, mid, gsum, theirs, landing,
+                 buf1, buf2, mid, gsum, spread, theirs, landing,
                  w_sem, in_sem, out_sem, send_sem, recv_sem):
     place = Place()
     links = Links(send_sem, recv_sem)
@@ -219,9 +279,9 @@
             for g in range(2):
                 out[g, place.z, place.y, place.x, start:start + size] = block[:, g * HD:(g + 1) * HD]
 
-    def gather(start, size, g):
+    def gather(how, start, size, g):
         rows = pl.ds(start, size)
-        return gather_rows(
+        return how(
             links, place,
             lambda z, y, x: kbuf.at[g, z, y, x, rows],
             lambda z, y, x: vbuf.at[g, z, y, x, rows],
@@ -229,7 +289,7 @@
 
     every = slice(None)
     project(0, 16)
-    first = gather(0, 16, every)
+    first = gather(gather_rows_late, 0, 16, every)
     next(first)
     links.landed(a, hall.at[low, lo], to_left)
     e = links.send(hall.at[low, lo], hall.at[far, lo], to_right)
@@ -239,43 +299,62 @@
     links.landed(c, hall.at[low, hi], to_left)
     links.landed(d, hall.at[high, lo], to_right)
     project(16, 32)
-    second = gather(16, 32, every)
+    second = gather(gather_rows_late, 16, 32, every)
+    next(second)
+    next(first)
     next(second)
     links.landed(e, hall.at[far, lo], to_left)
     links.landed(f, hall.at[far, hi], to_right)
     project(48, 16)
-    third, fourth = gather(48, 16, 0), gather(48, 16, 1)
+    third, fourth = gather(gather_rows, 48, 16, 0), gather(gather_rows, 48, 16, 1)
     next(third)
-    next(second)
     next(fourth)
     swap = swap_columns(links, place, hall, mine, turned, cols)
     next(swap)
+    next(second)
+    next(third)
     for load in loads:
         load.wait()
     next(first, None)
-    next(third)
     next(second, None)
     next(third, None)
 
-    def terms(ref, g):
-        return lambda z, y, x: ref.at[g, z, y, x]
-
-    def put(g):
-        def store(which, total):
-            gsum[g, place.y, place.x, place.z, :, which * HD:(which + 1) * HD] = total
-        return store
-
-    def reduce(g):
-        return reduce_rows(links, place, terms(gk, g), terms(gv, g), buf1.at[g], buf2.at[g], mid.at[g], put(g))
-
-    def regather(g):
-        return gather_rows(
+    count = cols.shape[4]
+    outs = (wk_out, wv_out)
+
+    def chain(g):
+        return run_chain(g, gsum.at[g], buf1.at[g], buf2.at[g], mid.at[g], theirs.at[g], landing.at[g])
+
+    def run_chain(g, total, first_landing, second_landing, between, own, last_landing):
+        def put(which, value):
+            total[which, along(place, "yx"[which], 0), place.z] = value
+
+        yield from reduce_rows(
             links, place,
-            lambda z, y, x: gsum.at[g, y, x, z, :, pl.ds(0, HD)],
-            lambda z, y, x: gsum.at[g, y, x, z, :, pl.ds(HD, HD)],
+            lambda z, y, x: gk.at[g, z, y, x],
+            lambda z, y, x: gv.at[g, z, y, x],
+            first_landing, second_landing, between, put,
         )
-
-    reduces = [reduce(0), reduce(1)]
+        yield from gather_plane(
+            links, place,
+            lambda z, y: total.at[0, y, z],
+            lambda z, x: total.at[1, x, z],
+        )
+        for which, axis in ((0, "x"), (1, "y")):
+            rhs = total[which].reshape(-1, HD)
+            product = jnp.dot(lhs[which], rhs, preferred_element_type=F32).astype(B16)
+            spread[g, which] = product.reshape(spread.shape[2:])
+            for core in range(2):
+                for s in range(4):
+                    k = along(place, axis, s)
+                    own[which, core, s] = spread[g, which, place.cores[core], k]
+
+        def done(which, value):
+            outs[which][:, g * HD:(g + 1) * HD] = value
+
+        yield from reduce_products(links, place, own, last_landing, done)
+
+    chains = [chain(0), chain(1)]
     causal = lax.broadcasted_iota(jnp.int32, (RLEN, RLEN), 1) <= lax.broadcasted_iota(jnp.int32, (RLEN, RLEN), 0)
 
     def block(b, _):
@@ -288,7 +367,7 @@
 
         @pl.when(b == 2)
         def _():
-            next(reduces[0])
+            next(chains[0])
             next(fourth, None)
 
         is_first = assign[r] == 0
@@ -296,13 +375,19 @@
         for src, dst in ((kbuf, kall), (vbuf, vall)):
             dst[b, :PLEN] = jnp.where(is_first, src[g, 0].reshape(PLEN, HD), src[g, 1].reshape(PLEN, HD))
         dkt = dvt = None
+
+        def scores(j):
+            s = lax.dot_general(qb[b, :, j * HD:(j + 1) * HD], kall[b], NT, preferred_element_type=F32)
+            return jnp.concatenate([s[:, :PLEN], jnp.where(causal, s[:, PLEN:], NEG_FILL)], axis=1)
+
+        following = scores(0)
         for j in range(GRP):
             lanes = slice(j * HD, (j + 1) * HD)
             q = qb[b, :, lanes]
-            k = kall[b]
             v = vall[b]
-            s = lax.dot_general(q, k, NT, preferred_element_type=F32)
-            s = jnp.concatenate([s[:, :PLEN], jnp.where(causal, s[:, PLEN:], NEG_FILL)], axis=1)
+            s = following
+            if j + 1 < GRP:
+                following = scores(j + 1)
             top = jnp.max(s, axis=1, keepdims=True)
             e = jnp.exp2((s - top) * SCALE_LOG2E)
             inv = 1.0 / jnp.sum(e, axis=1, keepdims=True)
@@ -324,7 +409,7 @@
             if j == 2:
                 @pl.when(b == 3)
                 def _():
-                    next(reduces[0])
+                    next(chains[0])
         dk = (dkt * SCALE).T
         dv = dvt.T
 
@@ -370,43 +455,22 @@
         store(4 * b + 2, drk.at[b], part(drk_hbm, b, HD))
         store(4 * b + 3, drv.at[b], part(drv_hbm, b, HD))
 
-    count = cols.shape[3]
-
-    def product(g):
-        rhs = gsum[g].reshape(NY * NX * NZ * gsum.shape[4], 2 * HD)
-        theirs[g] = jnp.dot(lhs[...], rhs, preferred_element_type=F32).reshape(2, count, 2 * HD)
-        return links.send(theirs.at[g, 1 - place.p], landing.at[g], place.core)
-
-    def finish(g, number):
-        links.landed(number, landing.at[g], place.core)
-        total = theirs[g, place.p] + landing[g]
-        wk_out[:, g * HD:(g + 1) * HD] = total[:, :HD]
-        wv_out[:, g * HD:(g + 1) * HD] = total[:, HD:]
-
-    next(reduces[1])
+    next(chains[1])
     late(0)
-    next(reduces[0], None)
-    regathers = [regather(0), regather(1)]
-    next(regathers[0])
+    next(chains[0])
+    next(swap, None)
+    for which in range(2):
+        for k in range(4):
+            lhs[which, :, k * HD:(k + 1) * HD] = cols[which, k].reshape(lhs.shape[1], HD)
     late(1)
-    next(swap, None)
-    for y in range(NY):
-        for x in range(NX):
-            at = (y * NX + x) * HD
-            lhs[:, at:at + HD] = cols[y, x].reshape(2 * count, HD)
-    next(reduces[1])
-    next(regathers[0])
+    next(chains[1])
+    next(chains[0])
     late(2)
-    next(reduces[1], None)
-    next(regathers[1])
+    next(chains[1])
     late(3)
-    next(regathers[1])
-    next(regathers[0], None)
-    first_product = product(0)
-    next(regathers[1], None)
-    second_product = product(1)
-    finish(0, first_product)
-    finish(1, second_product)
+    next(chains[1])
+    next(chains[0], None)
+    next(chains[1], None)
     for copy in stores:
         copy.wait()
 
@@ -434,7 +498,7 @@
             V((tall, depth), B16), V((depth, width), B16), V((depth, width), B16),
             V((2, NZ, NY, NX, tall, HD), B16), V((2, NZ, NY, NX, tall, HD), B16),
             V((2, NZ, tall, depth // 4), B16), V((2, NY, NX, count, HD), B16),
-            V((NY, NX, 2, count, HD), B16), V((2 * count, NY * NX * HD), B16),
+            V((2, 4, 2, 4, count, HD), B16), V((2, 8 * count, 4 * HD), B16),
             V((BLOCKS, RLEN, wide), B16), V((BLOCKS, RLEN, wide), B16),
             V((BLOCKS, keys, HD), B16), V((BLOCKS, keys, HD), B16),
             V((BLOCKS, RLEN, wide), B16), V((BLOCKS, RLEN, wide), B16),
@@ -443,8 +507,8 @@
             V((2, PLEN, HD), F32), V((2, PLEN, HD), F32),
             V((2, NZ, NY, NX, tall, HD), B16), V((2, NZ, NY, NX, tall, HD), B16),
             V((2, 2, 3, NZ, 4, tall, HD), B16), V((2, 2, 7, tall, HD), B16), V((2, 2, NZ, 4, tall, HD), B16),
-            V((2, NY, NX, NZ, tall, 2 * HD), B16),
-            V((2, 2, count, 2 * HD), F32), V((2, count, 2 * HD), F32),
+            V((2, 2, 4, NZ, tall, HD), B16), V((2, 2, 2, 4, count, HD), B16),
+            V((2, 2, 2, 4, count, HD), B16), V((2, 2, 7, count, HD), B16),
             pltpu.SemaphoreType.DMA((2,)), pltpu.SemaphoreType.DMA((4 * BLOCKS,)), pltpu.SemaphoreType.DMA((4 * BLOCKS,)),
             pltpu.SemaphoreType.DMA((copies,)), pltpu.SemaphoreType.DMA((copies,)),
         ],

time: 98.4 us -> 94.3 us (0.958)
  Pallas kernels: 97.4 us -> 93.4 us
    pallas_call x1, Pallas kernels: 94.5 us -> 90.4 us  [layer(): pl.pallas_call(layer_kernel, in_specs=[sm, sm, vm] + [hbm] * 6, out_specs...]
where the time goes in v2:
time: 94.3 us; the launch traced here: 94.2 us
  Pallas kernels  93.4 us (99%)
    pallas_call x1, Pallas kernels, layer(): pl.pallas_call(layer_kernel, in_specs=[sm, sm, vm] + [hbm] * 6, out_specs...  90.4 us
    pallas_call x1, Pallas kernels, hand_over(): pl.pallas_call(hand_over_kernel, in_specs=[hbm] * len(arrays), out_specs=...  2.99 us

profile of v2, /device:TPU:1, one launch (start us, length us, event | category | flops | bytes accessed | tf_op | source)
XLA Modules:
  0.0 94.2 jit_solution(5318143709444913814)
XLA Ops:
  0.6 90.4 %layer.1 = (bf16[2,256,1280]{2,1,0:T(8,128)(2,1)}, bf16[2,256,1280]{2,1,0:T(8,128)(2,1)}, bf16[2,256,256]{2,1,0:T(8,128)(2,1)}, bf16[2,256,256]{2,1,0:T(8,128)(2...) custom-call(s32[2]{0:T(128)} %lengths.1, s32[2]{0:T(128)} %assign.1, bf16[16,5120]{1,0:T(8,128)(2,1)} %hid.1, ...), custom_call_target="tpu_custom_call" | custom-call | tf_op jit(solution)/shard_map/layer/pallas_call | solution.py:492
  91.0 3.0 %hand_over.1 = (bf16[2,256,1280]{2,1,0:T(8,128)(2,1)}, bf16[2,256,1280]{2,1,0:T(8,128)(2,1)}, bf16[2,256,256]{2,1,0:T(8,128)(2,1)}, bf16[2,256,256]{2,1,0:T(8,12...) custom-call(bf16[2,256,1280]{2,1,0:T(8,128)(2,1)} %get-tuple-element.12.refs_0_, ...), custom_call_target="tpu_custom_call" | custom-call | tf_op jit(solution)/shard_map/hand_over/pallas_call | solution.py:542

commit v3 on v2

--- a/solution.py
+++ b/solution.py
@@ -299,14 +299,14 @@
     links.landed(c, hall.at[low, hi], to_left)
     links.landed(d, hall.at[high, lo], to_right)
     project(16, 32)
-    second = gather(gather_rows_late, 16, 32, every)
+    second = gather(gather_rows_late, 16, 32, 0)
     next(second)
     next(first)
     next(second)
     links.landed(e, hall.at[far, lo], to_left)
     links.landed(f, hall.at[far, hi], to_right)
     project(48, 16)
-    third, fourth = gather(gather_rows, 48, 16, 0), gather(gather_rows, 48, 16, 1)
+    third, fourth = gather(gather_rows, 48, 16, 0), gather(gather_rows, 16, 48, 1)
     next(third)
     next(fourth)
     swap = swap_columns(links, place, hall, mine, turned, cols)
@@ -318,6 +318,7 @@
     next(first, None)
     next(second, None)
     next(third, None)
+    next(fourth)
 
     count = cols.shape[4]
     outs = (wk_out, wv_out)
@@ -362,7 +363,6 @@
 
         @pl.when(b == 1)
         def _():
-            next(fourth)
             next(swap)
 
         @pl.when(b == 2)
@@ -406,10 +406,6 @@
             vt = lax.dot_general(grad, e_low[:, :PLEN], TN, preferred_element_type=F32)
             dkt = kt if j == 0 else dkt + kt
             dvt = vt if j == 0 else dvt + vt
-            if j == 2:
-                @pl.when(b == 3)
-                def _():
-                    next(chains[0])
         dk = (dkt * SCALE).T
         dv = dvt.T
 
@@ -456,20 +452,21 @@
         store(4 * b + 3, drv.at[b], part(drv_hbm, b, HD))
 
     next(chains[1])
+    next(chains[0])
     late(0)
+    late(1)
+    late(2)
     next(chains[0])
+    next(chains[1])
     next(swap, None)
     for which in range(2):
         for k in range(4):
             lhs[which, :, k * HD:(k + 1) * HD] = cols[which, k].reshape(lhs.shape[1], HD)
-    late(1)
-    next(chains[1])
+    late(3)
     next(chains[0])
-    late(2)
-    next(chains[1])
-    late(3)
     next(chains[1])
     next(chains[0], None)
+    next(chains[1])
     next(chains[1], None)
     for copy in stores:
         copy.wait()

time: 94.3 us -> 90.3 us (0.958)
  Pallas kernels: 93.4 us -> 89.3 us
    pallas_call x1, Pallas kernels: 90.4 us -> 86.4 us  [layer(): pl.pallas_call(layer_kernel, in_specs=[sm, sm, vm] + [hbm] * 6, out_specs...]
where the time goes in v3:
time: 90.3 us; the launch traced here: 90.1 us
  Pallas kernels  89.3 us (99%)
    pallas_call x1, Pallas kernels, layer(): pl.pallas_call(layer_kernel, in_specs=[sm, sm, vm] + [hbm] * 6, out_specs...  86.4 us
    pallas_call x1, Pallas kernels, hand_over(): pl.pallas_call(hand_over_kernel, in_specs=[hbm] * len(arrays), out_specs=...  2.99 us

profile of v3, /device:TPU:1, one launch (start us, length us, event | category | flops | bytes accessed | tf_op | source)
XLA Modules:
  0.0 90.1 jit_solution(8614961601946118657)
XLA Ops:
  0.6 86.4 %layer.1 = (bf16[2,256,1280]{2,1,0:T(8,128)(2,1)}, bf16[2,256,1280]{2,1,0:T(8,128)(2,1)}, bf16[2,256,256]{2,1,0:T(8,128)(2,1)}, bf16[2,256,256]{2,1,0:T(8,128)(2...) custom-call(s32[2]{0:T(128)} %lengths.1, s32[2]{0:T(128)} %assign.1, bf16[16,5120]{1,0:T(8,128)(2,1)} %hid.1, ...), custom_call_target="tpu_custom_call" | custom-call | tf_op jit(solution)/shard_map/layer/pallas_call | solution.py:489
  87.0 3.0 %hand_over.1 = (bf16[2,256,1280]{2,1,0:T(8,128)(2,1)}, bf16[2,256,1280]{2,1,0:T(8,128)(2,1)}, bf16[2,256,256]{2,1,0:T(8,128)(2,1)}, bf16[2,256,256]{2,1,0:T(8,12...) custom-call(bf16[2,256,1280]{2,1,0:T(8,128)(2,1)} %get-tuple-element.12.refs_0_, ...), custom_call_target="tpu_custom_call" | custom-call | tf_op jit(solution)/shard_map/hand_over/pallas_call | solution.py:539

commit v4 on v3

--- a/solution.py
+++ b/solution.py
@@ -406,6 +406,10 @@
             vt = lax.dot_general(grad, e_low[:, :PLEN], TN, preferred_element_type=F32)
             dkt = kt if j == 0 else dkt + kt
             dvt = vt if j == 0 else dvt + vt
+            if j == 3:
+                @pl.when(b == 3)
+                def _():
+                    next(chains[0])
         dk = (dkt * SCALE).T
         dv = dvt.T
 
@@ -452,11 +456,10 @@
         store(4 * b + 3, drv.at[b], part(drv_hbm, b, HD))
 
     next(chains[1])
+    late(0)
     next(chains[0])
-    late(0)
     late(1)
     late(2)
-    next(chains[0])
     next(chains[1])
     next(swap, None)
     for which in range(2):

time: 90.3 us -> 89.1 us (0.987)
  Pallas kernels: 89.3 us -> 88.2 us
    pallas_call x1, Pallas kernels: 86.4 us -> 85.2 us  [layer(): pl.pallas_call(layer_kernel, in_specs=[sm, sm, vm] + [hbm] * 6, out_specs...]
where the time goes in v4:
time: 89.1 us; the launch traced here: 89 us
  Pallas kernels  88.2 us (99%)
    pallas_call x1, Pallas kernels, layer(): pl.pallas_call(layer_kernel, in_specs=[sm, sm, vm] + [hbm] * 6, out_specs...  85.2 us
    pallas_call x1, Pallas kernels, hand_over(): pl.pallas_call(hand_over_kernel, in_specs=[hbm] * len(arrays), out_specs=...  2.99 us

profile of v4, /device:TPU:1, one launch (start us, length us, event | category | flops | bytes accessed | tf_op | source)
XLA Modules:
  0.0 89.0 jit_solution(1396229780533216076)
XLA Ops:
  0.6 85.2 %layer.1 = (bf16[2,256,1280]{2,1,0:T(8,128)(2,1)}, bf16[2,256,1280]{2,1,0:T(8,128)(2,1)}, bf16[2,256,256]{2,1,0:T(8,128)(2,1)}, bf16[2,256,256]{2,1,0:T(8,128)(2...) custom-call(s32[2]{0:T(128)} %lengths.1, s32[2]{0:T(128)} %assign.1, bf16[16,5120]{1,0:T(8,128)(2,1)} %hid.1, ...), custom_call_target="tpu_custom_call" | custom-call | tf_op jit(solution)/shard_map/layer/pallas_call | solution.py:492
  85.8 3.0 %hand_over.1 = (bf16[2,256,1280]{2,1,0:T(8,128)(2,1)}, bf16[2,256,1280]{2,1,0:T(8,128)(2,1)}, bf16[2,256,256]{2,1,0:T(8,128)(2,1)}, bf16[2,256,256]{2,1,0:T(8,12...) custom-call(bf16[2,256,1280]{2,1,0:T(8,128)(2,1)} %get-tuple-element.12.refs_0_, ...), custom_call_target="tpu_custom_call" | custom-call | tf_op jit(solution)/shard_map/hand_over/pallas_call | solution.py:542
